TPU v7x, 128 devices: a whole 4x4x4 slice. The times are simulated.
128 devices in a mesh: gx: 8 (over x, z_lo), gy: 16 (over z_hi, y, core).
Axes of the slice: x: 4, y: 4, z: 4 (z_hi: 2, z_lo: 2; z = z_hi * 2 + z_lo), core: 2. Of those that a mesh axis runs over, the one named last changes fastest.
Arguments:
- tangents: float32 [5, 3, 32, 64, 2048], P(None, None, 'gx', None, 'gy'), may hold values from -72 to 72, as said below
- base_flow: float32 [2, 3, 32, 64, 2048], P(None, None, 'gx', None, 'gy'), may hold values from -4 to 4
- objective_weight: float32 [3, 32, 64, 2048], P(None, 'gx', None, 'gy'), may hold values from -5.6 to 5.6, as said below
Outputs:
- renormed: float32 [5, 3, 32, 64, 2048], P(None, None, 'gx', None, 'gy')
- rfactor: float32 [4, 4], replicated
- coefficients: float32 [4], replicated
- objective: float32 [5], replicated
Inputs may be any that keep to these rules, and one draw needn't show every extreme that they name: `tangents`: finite tangent velocities. `objective_weight`: finite weights.
All inputs are finite; a program needn't handle non-finite values.
Results may differ from a plain program's by a relative error of at most 0.000077.
Values sent between devices are 32-bit elements; how exact they have to be, the bound alone decides.
No kernel may reach another device: no remote copies, remote signals or barrier semaphores. Data moves between devices by JAX's collectives and lax.ppermute only.
A program may use at most 128 MiB of HBM per device.

v0:
```python
import jax
import jax.numpy as jnp
from jax import lax
from jax.sharding import PartitionSpec as P

time_step = 0.2
viscosity = 0.05


def padded_2(cells, sides, width):
    for axis, dim in sides:
        count = lax.axis_size(axis)
        head = lax.slice_in_dim(cells, 0, width, axis=dim)
        tail = lax.slice_in_dim(cells, cells.shape[dim] - width, cells.shape[dim], axis=dim)
        cells = jnp.concatenate(
            [
                lax.ppermute(tail, axis, [(i, (i + 1) % count) for i in range(count)]),
                cells,
                lax.ppermute(head, axis, [((i + 1) % count, i) for i in range(count)]),
            ],
            axis=dim,
        )
    return cells


def take_cells(values_in, step_x, step_y, step_z):
    width_x = values_in.shape[-3] - 2
    width_y = values_in.shape[-1] - 2
    if step_z != 0:
        padded = jnp.pad(values_in, [(0, 0)] * (values_in.ndim - 2) + [(1, 1), (0, 0)])
        values_in = padded[..., 1 + step_z : 1 + step_z + values_in.shape[-2], :]
    return values_in[..., 1 + step_x : 1 + step_x + width_x, :, 1 + step_y : 1 + step_y + width_y]


def gradients(values_in):
    return (
        0.5 * (take_cells(values_in, 1, 0, 0) - take_cells(values_in, -1, 0, 0)),
        0.5 * (take_cells(values_in, 0, 1, 0) - take_cells(values_in, 0, -1, 0)),
        0.5 * (take_cells(values_in, 0, 0, 1) - take_cells(values_in, 0, 0, -1)),
    )


def laplacian(values_in):
    summed = take_cells(values_in, 1, 0, 0) + take_cells(values_in, -1, 0, 0)
    summed = summed + take_cells(values_in, 0, 1, 0) + take_cells(values_in, 0, -1, 0)
    summed = summed + take_cells(values_in, 0, 0, 1) + take_cells(values_in, 0, 0, -1)
    return summed - 6.0 * take_cells(values_in, 0, 0, 0)


def rate_all(wide, flow_wide, source_mask):
    field_grad = gradients(wide)
    flow_grad = gradients(flow_wide)
    field_centre = take_cells(wide, 0, 0, 0)
    flow_centre = take_cells(flow_wide, 0, 0, 0)
    advect = (
        flow_centre[0] * field_grad[0]
        + flow_centre[1] * field_grad[1]
        + flow_centre[2] * field_grad[2]
    )
    produce = (
        field_centre[:, 0:1] * flow_grad[0]
        + field_centre[:, 1:2] * flow_grad[1]
        + field_centre[:, 2:3] * flow_grad[2]
    )
    return -advect - produce + viscosity * laplacian(wide) + source_mask * laplacian(flow_wide)


def with_rims(fields, flow_in):
    joined = jnp.concatenate([fields.reshape((15,) + fields.shape[2:]), flow_in], 0)
    padded = padded_2(joined, (("gx", 1), ("gy", 3)), 1)
    return (padded[:15].reshape((5, 3) + padded.shape[1:]), padded[15:])


def lower_inverse(lower_factor):
    count_rows = lower_factor.shape[0]
    identity_rows = jnp.eye(count_rows, dtype=lower_factor.dtype)
    inverse_rows = []
    for row_index in range(count_rows):
        row_value = identity_rows[row_index]
        for column in range(row_index):
            row_value = row_value - lower_factor[row_index, column] * inverse_rows[column]
        inverse_rows.append(row_value / lower_factor[row_index, row_index])
    return jnp.stack(inverse_rows)


def per_device(tangents, base_flow, objective_weight):
    highest = lax.Precision.HIGHEST
    local_shape = tangents.shape
    source_mask = (jnp.arange(5) == 4).astype(jnp.float32).reshape(5, 1, 1, 1, 1)
    wide, flow_wide = with_rims(tangents, base_flow[0])
    first = tangents + time_step * rate_all(wide, flow_wide, source_mask)
    wide, flow_wide = with_rims(first, base_flow[1])
    second_rate = rate_all(wide, flow_wide, source_mask)
    second = 0.5 * (tangents + first + time_step * second_rate)
    first_local = jnp.sum(objective_weight[None] * first, axis=(1, 2, 3, 4))
    second_local = jnp.sum(objective_weight[None] * second, axis=(1, 2, 3, 4))
    matrix = second.reshape(5, -1)
    gram_local = jnp.dot(matrix, matrix.T, precision=highest)
    total_cells = (
        local_shape[2] * local_shape[3] * local_shape[4] * lax.axis_size("gx") * lax.axis_size("gy")
    )
    first_total = lax.psum(first_local, ("gx", "gy"))
    gram_total, carried_total = lax.psum((gram_local, second_local), ("gx", "gy"))
    objective = 0.5 * (first_total + carried_total) / total_cells
    gram_matrix = gram_total / (3.0 * total_cells)
    lower_factor = jnp.linalg.cholesky(gram_matrix[:4, :4])
    inverse = lower_inverse(lower_factor)
    coefficients = jnp.dot(inverse, gram_matrix[:4, 4], precision=highest)
    ortho = jnp.dot(inverse, matrix[:4], precision=highest)
    last_row = matrix[4] - jnp.dot(coefficients, ortho, precision=highest)
    renormed = jnp.concatenate([ortho, last_row[None]], 0).reshape(local_shape)
    return (renormed, lower_factor.T, coefficients, objective)


def solution(mesh):
    placed = (
        P(None, None, "gx", None, "gy"),
        P(None, None, "gx", None, "gy"),
        P(None, "gx", None, "gy"),
    )
    return jax.shard_map(
        per_device,
        mesh=mesh,
        in_specs=placed,
        out_specs=(P(None, None, "gx", None, "gy"), P(), P(), P()),
        check_vma=False,
    )
```

profile of v0, /device:TPU:1, one launch (start us, length us, event | category | flops | bytes accessed | tf_op | source)
XLA Modules:
  0.0 235.3 jit_solution(13409901271503922823)
XLA Ops:
  0.6 1.2 slice_bitcast_fusion.7
  1.8 1.4 pad_maximum_fusion.8
  3.3 4.7 %collective-permute-start.1 = (f32[18,1,64,128]{3,2,1,0:T(8,128)S(1)}, f32[18,1,64,128]{3,2,1,0:T(8,128)S(1)}, u32[]{:S(2)}, u32[]{:S(2)}) collective-permute-start(f32[18,1,64,128]{3,2,1,0:T(8,128)S(1)} %get-tuple-element.57), channel_id=1, source_target_pairs={{16,0},{32,16},{48,32},{64,48},{80,64},{96,80},{112,96},{0,112},{1... | collective-permute-start | bytes 1769480 | tf_op jit(solution)/shard_map/ppermute | solution.py:19
  8.0 0.9 multiply_bitcast_fusion.2
  8.9 22.6 %collective-permute-done.1 = f32[18,1,64,128]{3,2,1,0:T(8,128)S(1)} collective-permute-done((f32[18,1,64,128]{3,2,1,0:T(8,128)S(1)}, f32[18,1,64,128]{3,2,1,0:T(8,128)S(1)}, u32[]{:S(2)}, u32[]{:S(2)}) %collective-permute-start.1) | collective-permute-done | bytes 589856 | tf_op jit(solution)/shard_map/ppermute | solution.py:19
  31.5 0.9 collective-permute-done
  32.4 0.8 copy-done.8
  33.2 0.3 pad_maximum_fusion.2
  33.5 4.1 %fusion.32 = (f32[18,6,64,1]{3,2,1,0:T(8,128)}, f32[18,6,64,1]{3,2,1,0:T(8,128)}) fusion(f32[18,6,64,128]{3,2,1,0:T(8,128)S(1)} %pad_maximum_fusion.2), kind=kLoop, calls=%fused_computation.119 | loop fusion | bytes 110592 | tf_op jit(solution)/shard_map/slice | solution.py:14
  37.6 3.0 %copy.69 = f32[18,6,64,1]{2,1,3,0:T(8,128)S(1)} copy(f32[18,6,64,1]{3,2,1,0:T(8,128)} %get-tuple-element.53) | data formatting | bytes 55296
  40.6 0.6 collective-permute-start.3
  41.2 3.6 %copy.68 = f32[18,6,64,1]{2,1,3,0:T(8,128)} copy(f32[18,6,64,1]{3,2,1,0:T(8,128)} %get-tuple-element.52) | data formatting | bytes 55296
  44.8 1.3 collective-permute-start.2
  46.1 3.2 %copy.52 = f32[18,6,64,1]{3,2,1,0:T(8,128)} copy(f32[18,6,64,1]{2,1,3,0:T(8,128)} %collective-permute-done.3) | data formatting | bytes 55296 | tf_op jit(solution)/shard_map/ppermute | solution.py:19
  49.2 2.3 collective-permute-done.2
  51.6 3.2 %copy.51 = f32[18,6,64,1]{3,2,1,0:T(8,128)} copy(f32[18,6,64,1]{2,1,3,0:T(8,128)} %collective-permute-done.2) | data formatting | bytes 55296 | tf_op jit(solution)/shard_map/ppermute | solution.py:17
  54.8 7.0 %pad_maximum_fusion = f32[18,6,64,130]{3,2,1,0:T(8,128)S(1)} fusion(f32[18,6,64,1]{3,2,1,0:T(8,128)} %copy.52, f32[18,1,64,128]{3,2,1,0:T(8,128)S(1)} %collective-permute-done.1, f32[3,4,64,128]{3,2,1,0:T(8,128)S(1)} %get-tuple-element.68, f32[15,4,64,128]{3,2,1,0:T(8,128)S(1)} %bitcast.73, f32[18,1,64,128]{3,2,1,0:T(8,128)} %copy-done.8, f32[18,6,64,1]{3,2,1,0:T(8,128)} %copy.51), kind=kLoop, calls=%fused_computation | loop fusion | flops 4492800 | bytes 7188480 | tf_op jit(solution)/shard_map/concatenate | solution.py:15
  61.8 0.7 slice.409
  62.6 0.6 slice_bitcast_fusion.5
  63.1 0.7 copy-done.5
  63.9 1.3 copy-done.3
  65.2 0.6 select_maximum_fusion.5
  65.9 0.5 subtract_multiply_fusion.5
  66.4 0.6 copy-done.11
  67.0 0.3 subtract_multiply_fusion.3
  67.4 3.8 %multiply_reduce_fusion.1 = (f32[5]{0:T(128)S(1)}, f32[5,3,4,64,128]{4,3,2,1,0:T(8,128)S(1)}) fusion(f32[3,4,64,128]{3,2,1,0:T(8,128)S(1)} %copy-done.14, f32[5,3,4,64,128]{4,3,2,1,0:T(8,128)S(1)} %copy-done, f32[3,4,64,128]{3,2,1,0:T(8,128)S(1)} %get-tuple-element.61, f32[5]{0:T(128)S(1)} %compare_convert_fusion, f32[5,3,6,64,130]{4,3,2,1,0:T(8,128)S(1)} %bitcast.84, ...), kind=kLoop, calls=%fused_computation.28 | loop fusion | flops 14745595 | bytes 23986708 | tf_op jit(solution)/shard_map/reduce_sum | solution.py:95
  71.4 2.0 collective-permute-start.5
  73.4 0.8 broadcast_multiply_fusion.1
  74.2 21.3 %collective-permute-done.5 = f32[18,1,64,128]{3,2,1,0:T(8,128)S(1)} collective-permute-done((f32[18,1,64,128]{3,2,1,0:T(8,128)S(1)}, f32[18,1,64,128]{3,2,1,0:T(8,128)S(1)}, u32[]{:S(2)}, u32[]{:S(2)}) %collective-permute-start.5) | collective-permute-done | bytes 589856 | tf_op jit(solution)/shard_map/ppermute | solution.py:19
  95.5 2.9 %collective-permute-done.4 = f32[18,1,64,128]{3,2,1,0:T(8,128)S(1)} collective-permute-done((f32[18,1,64,128]{3,2,1,0:T(8,128)S(1)}, f32[18,1,64,128]{3,2,1,0:T(8,128)S(1)}, u32[]{:S(2)}, u32[]{:S(2)}) %collective-permute-start.4) | collective-permute-done | bytes 589856 | tf_op jit(solution)/shard_map/ppermute | solution.py:17
  98.4 0.4 pad_maximum_fusion.3
  98.8 4.1 %fusion.31 = (f32[18,6,64,1]{3,2,1,0:T(8,128)}, f32[18,6,64,1]{3,2,1,0:T(8,128)}) fusion(f32[18,6,64,128]{3,2,1,0:T(8,128)S(1)} %pad_maximum_fusion.3), kind=kLoop, calls=%fused_computation.118 | loop fusion | bytes 110592 | tf_op jit(solution)/shard_map/slice | solution.py:14
  102.9 3.6 %copy.71 = f32[18,6,64,1]{2,1,3,0:T(8,128)} copy(f32[18,6,64,1]{3,2,1,0:T(8,128)} %get-tuple-element.48) | data formatting | bytes 55296
  106.5 1.6 collective-permute-start.7
  108.1 3.6 %copy.70 = f32[18,6,64,1]{2,1,3,0:T(8,128)} copy(f32[18,6,64,1]{3,2,1,0:T(8,128)} %get-tuple-element.47) | data formatting | bytes 55296
  111.9 3.2 %copy.58 = f32[18,6,64,1]{3,2,1,0:T(8,128)} copy(f32[18,6,64,1]{2,1,3,0:T(8,128)} %collective-permute-done.7) | data formatting | bytes 55296 | tf_op jit(solution)/shard_map/ppermute | solution.py:19
  115.0 2.5 %collective-permute-done.6 = f32[18,6,64,1]{2,1,3,0:T(8,128)} collective-permute-done((f32[18,6,64,1]{2,1,3,0:T(8,128)}, f32[18,6,64,1]{2,1,3,0:T(8,128)}, u32[]{:S(2)}, u32[]{:S(2)}) %collective-permute-start.6) | collective-permute-done | bytes 27680 | tf_op jit(solution)/shard_map/ppermute | solution.py:17
  117.6 3.2 %copy.57 = f32[18,6,64,1]{3,2,1,0:T(8,128)} copy(f32[18,6,64,1]{2,1,3,0:T(8,128)} %collective-permute-done.6) | data formatting | bytes 55296 | tf_op jit(solution)/shard_map/ppermute | solution.py:17
  120.8 7.2 %pad_maximum_fusion.1 = f32[18,6,64,130]{3,2,1,0:T(8,128)S(1)} fusion(f32[18,6,64,1]{3,2,1,0:T(8,128)} %copy.58, f32[18,1,64,128]{3,2,1,0:T(8,128)S(1)} %collective-permute-done.5, f32[3,4,64,128]{3,2,1,0:T(8,128)S(1)} %get-tuple-element.69, f32[15,4,64,128]{3,2,1,0:T(8,128)} %bitcast.78, f32[18,1,64,128]{3,2,1,0:T(8,128)S(1)} %collective-permute-done.4, ...), kind=kLoop, calls=%fused_computation.1 | loop fusion | flops 4492800 | bytes 7188480 | tf_op jit(solution)/shard_map/concatenate | solution.py:15
  128.0 0.4 slice.422
  128.5 0.6 slice_bitcast_fusion.2
  129.0 1.0 copy-done.4
  130.0 1.1 copy-done.6
  131.1 0.7 copy-done.2
  131.8 0.6 select_maximum_fusion
  132.4 1.2 subtract_multiply_fusion.2
  133.6 0.3 subtract_multiply_fusion
  133.9 0.6 copy-done.13
  134.7 4.7 %multiply_reduce_fusion = (f32[5]{0:T(128)S(1)}, f32[5,3,4,64,128]{4,3,2,1,0:T(8,128)S(1)}) fusion(f32[3,4,64,128]{3,2,1,0:T(8,128)S(1)} %copy-done.15, f32[3,4,64,128]{3,2,1,0:T(8,128)S(1)} %get-tuple-element.59, f32[5]{0:T(128)S(1)} %compare_convert_fusion, f32[5,3,6,64,130]{4,3,2,1,0:T(8,128)S(1)} %bitcast.82, ...), kind=kLoop, calls=%fused_computation.27 | loop fusion | flops 15237115 | bytes 25952788 | tf_op jit(solution)/shard_map/reduce_sum | solution.py:96
  139.5 0.2 broadcast_multiply_fusion
  139.6 6.8 %fusion.18 = f32[5,5]{0,1:T(8,128)S(1)} fusion(f32[5,3,4,64,128]{4,3,2,1,0:T(8,128)S(1)} %broadcast_multiply_fusion), kind=kOutput, calls=%fused_computation.43 | convolution fusion | flops 29491200 | bytes 1966180 | tf_op jit(solution)/shard_map/dot_general | solution.py:98
  146.6 68.4 %all-reduce.4 = (f32[5,5]{0,1:T(8,128)S(1)}, f32[5]{0:T(128)S(1)}) all-reduce(f32[5,5]{0,1:T(8,128)S(1)} %fusion.18, f32[5]{0:T(128)S(1)} %add.167), channel_id=1, replica_groups=mesh['gx'=8,'gy'=16] {'gx','gy'}, use_global_device_ids=true, to_apply=%region_0.1 | all-reduce | flops 30 | bytes 240 | tf_op jit(solution)/shard_map/psum | solution.py:103
  215.1 0.4 cholesky.14
  215.5 0.6 compare_reduce_fusion
  216.2 0.6 select_select_fusion
  216.8 0.7 fusion.35
  217.5 0.7 fusion.33
  218.2 6.3 %subtract_divide_fusion = (f32[1,4]{1,0:T(1,128)S(1)}, f32[1,4]{1,0:T(1,128)S(1)}, f32[1,4]{1,0:T(1,128)S(1)}, f32[1,4]{1,0:T(1,128)S(1)}) fusion(f32[4,4]{1,0:T(4,128)S(1)} %fusion.22, f32[]{:T(128)} %bitcast.29, f32[]{:T(128)} %bitcast.28, f32[]{:T(128)} %bitcast.27, f32[]{:T(128)} %bitcast.26, f32[]{:T(128)} %bitcast.25, f32[]{:T(128)} %bitcast.24, ...), kind=kLoop, calls=%fused_computation.109 | loop fusion | flops 64 | bytes 168 | tf_op jit(solution)/shard_map/div | solution.py:82
  224.6 3.5 %fusion.14 = f32[4,98304]{1,0:T(4,128)S(1)} fusion(f32[1,4,768,128]{3,2,1,0:T(8,128)S(1)} %bitcast.87, f32[1,4]{1,0:T(1,128)S(1)} %get-tuple-element.18, f32[1,4]{1,0:T(1,128)S(1)} %get-tuple-element.19, f32[1,4]{1,0:T(1,128)S(1)} %get-tuple-element.20, f32[1,4]{1,0:T(1,128)S(1)} %get-tuple-element.21), kind=kOutput, calls=%fused_computation.29 | convolution fusion | flops 18874416 | bytes 3145792 | tf_op jit(solution)/shard_map/dot_general | solution.py:109
  228.1 3.4 %fusion.23 = f32[1,98304]{1,0:T(1,128)} fusion(f32[4,98304]{1,0:T(4,128)S(1)} %fusion.14, f32[1,4]{1,0:T(1,128)S(1)} %fusion.25), kind=kOutput, calls=%fused_computation.107 | convolution fusion | flops 4718592 | bytes 1966096 | tf_op jit(solution)/shard_map/dot_general | solution.py:110
  231.7 0.7 copy.65
  232.3 0.5 broadcast_multiply_fusion.3
  232.9 1.0 sub.109
  233.9 1.4 pad_maximum_fusion.4
  (53 shorter events, 1.3 us)
Async XLA Ops:
  1.8 6.2 %copy-start.10 = (f32[2,3,4,64,128]{4,3,2,1,0:T(8,128)S(1)}, f32[2,3,4,64,128]{4,3,2,1,0:T(8,128)}, u32[]{:S(2)}) copy-start(f32[2,3,4,64,128]{4,3,2,1,0:T(8,128)} %param.4) | copy-start | bytes 2359300
  1.8 31.4 %copy-start = (f32[5,3,4,64,128]{4,3,2,1,0:T(8,128)S(1)}, f32[5,3,4,64,128]{4,3,2,1,0:T(8,128)}, u32[]{:S(2)}) copy-start(f32[5,3,4,64,128]{4,3,2,1,0:T(8,128)} %param.3) | copy-start | bytes 5898244
  3.3 28.2 %collective-permute-start.1 = (f32[18,1,64,128]{3,2,1,0:T(8,128)S(1)}, f32[18,1,64,128]{3,2,1,0:T(8,128)S(1)}, u32[]{:S(2)}, u32[]{:S(2)}) collective-permute-start(f32[18,1,64,128]{3,2,1,0:T(8,128)S(1)} %get-tuple-element.57), channel_id=1, source_target_pairs={{16,0},{32,16},{48,32},{64,48},{80,64},{96,80},{112,96},{0,112},{1... | collective-permute-start | bytes 1769480 | tf_op jit(solution)/shard_map/ppermute | solution.py:19
  8.0 24.4 %collective-permute-start = (f32[18,1,64,128]{3,2,1,0:T(8,128)S(1)}, f32[18,1,64,128]{3,2,1,0:T(8,128)S(1)}, u32[]{:S(2)}, u32[]{:S(2)}) collective-permute-start(f32[18,1,64,128]{3,2,1,0:T(8,128)S(1)} %get-tuple-element.56), channel_id=1, source_target_pairs={{0,16},{16,32},{32,48},{48,64},{64,80},{80,96},{96,112},{112,0},{1... | collective-permute-start | bytes 1769480 | tf_op jit(solution)/shard_map/ppermute | solution.py:17
  32.4 0.8 copy-start.8
  40.6 5.4 %collective-permute-start.3 = (f32[18,6,64,1]{2,1,3,0:T(8,128)S(1)}, f32[18,6,64,1]{2,1,3,0:T(8,128)}, u32[]{:S(2)}, u32[]{:S(2)}) collective-permute-start(f32[18,6,64,1]{2,1,3,0:T(8,128)S(1)} %copy.69), channel_id=1, source_target_pairs={{1,0},{2,1},{3,2},{4,3},{5,4},{6,5},{7,6},{8,7},{9,8},{10,9},{11,1... | collective-permute-start | bytes 82952 | tf_op jit(solution)/shard_map/ppermute | solution.py:19
  44.8 6.8 %collective-permute-start.2 = (f32[18,6,64,1]{2,1,3,0:T(8,128)}, f32[18,6,64,1]{2,1,3,0:T(8,128)}, u32[]{:S(2)}, u32[]{:S(2)}) collective-permute-start(f32[18,6,64,1]{2,1,3,0:T(8,128)} %copy.68), channel_id=1, source_target_pairs={{0,1},{1,2},{2,3},{3,4},{4,5},{5,6},{6,7},{7,8},{8,9},{9,10},{10,1... | collective-permute-start | bytes 82952 | tf_op jit(solution)/shard_map/ppermute | solution.py:17
  61.8 2.0 copy-start.5
  61.8 2.1 copy-start.9
  62.6 2.7 %copy-start.3 = (f32[18,6,64,1]{3,2,1,0:T(8,128)S(1)}, f32[18,6,64,1]{3,2,1,0:T(8,128)}, u32[]{:S(2)}) copy-start(f32[18,6,64,1]{3,2,1,0:T(8,128)} %copy.52) | copy-start | bytes 82948
  65.8 1.1 copy-start.11
  66.3 1.1 copy-start.14
  66.3 1.1 copy-start.18
  66.3 1.1 copy-start.19
  71.3 27.1 %copy-start.1 = (f32[5,3,4,64,128]{4,3,2,1,0:T(8,128)}, f32[5,3,4,64,128]{4,3,2,1,0:T(8,128)S(1)}, u32[]{:S(2)}) copy-start(f32[5,3,4,64,128]{4,3,2,1,0:T(8,128)S(1)} %get-tuple-element.25) | copy-start | bytes 5898244
  71.4 24.1 %collective-permute-start.5 = (f32[18,1,64,128]{3,2,1,0:T(8,128)S(1)}, f32[18,1,64,128]{3,2,1,0:T(8,128)S(1)}, u32[]{:S(2)}, u32[]{:S(2)}) collective-permute-start(f32[18,1,64,128]{3,2,1,0:T(8,128)S(1)} %get-tuple-element.55), channel_id=1, source_target_pairs={{16,0},{32,16},{48,32},{64,48},{80,64},{96,80},{112,96},{0,112},{1... | collective-permute-start | bytes 1769480 | tf_op jit(solution)/shard_map/ppermute | solution.py:19
  73.4 25.0 %collective-permute-start.4 = (f32[18,1,64,128]{3,2,1,0:T(8,128)S(1)}, f32[18,1,64,128]{3,2,1,0:T(8,128)S(1)}, u32[]{:S(2)}, u32[]{:S(2)}) collective-permute-start(f32[18,1,64,128]{3,2,1,0:T(8,128)S(1)} %get-tuple-element.54), channel_id=1, source_target_pairs={{0,16},{16,32},{32,48},{48,64},{64,80},{80,96},{96,112},{112,0},{1... | collective-permute-start | bytes 1769480 | tf_op jit(solution)/shard_map/ppermute | solution.py:17
  106.5 5.4 %collective-permute-start.7 = (f32[18,6,64,1]{2,1,3,0:T(8,128)}, f32[18,6,64,1]{2,1,3,0:T(8,128)}, u32[]{:S(2)}, u32[]{:S(2)}) collective-permute-start(f32[18,6,64,1]{2,1,3,0:T(8,128)} %copy.71), channel_id=1, source_target_pairs={{1,0},{2,1},{3,2},{4,3},{5,4},{6,5},{7,6},{8,7},{9,8},{10,9},{11,1... | collective-permute-start | bytes 82952 | tf_op jit(solution)/shard_map/ppermute | solution.py:19
  111.7 5.9 %collective-permute-start.6 = (f32[18,6,64,1]{2,1,3,0:T(8,128)}, f32[18,6,64,1]{2,1,3,0:T(8,128)}, u32[]{:S(2)}, u32[]{:S(2)}) collective-permute-start(f32[18,6,64,1]{2,1,3,0:T(8,128)} %copy.70), channel_id=1, source_target_pairs={{0,1},{1,2},{2,3},{3,4},{4,5},{5,6},{6,7},{7,8},{8,9},{9,10},{10,1... | collective-permute-start | bytes 82952 | tf_op jit(solution)/shard_map/ppermute | solution.py:17
  128.0 2.0 copy-start.4
  128.0 3.1 %copy-start.6 = (f32[18,6,64,1]{3,2,1,0:T(8,128)S(1)}, f32[18,6,64,1]{3,2,1,0:T(8,128)}, u32[]{:S(2)}) copy-start(f32[18,6,64,1]{3,2,1,0:T(8,128)} %copy.57) | copy-start | bytes 82948
  128.5 3.3 %copy-start.2 = (f32[5,3,4,64,128]{4,3,2,1,0:T(8,128)S(1)}, f32[5,3,4,64,128]{4,3,2,1,0:T(8,128)}, u32[]{:S(2)}) copy-start(f32[5,3,4,64,128]{4,3,2,1,0:T(8,128)} %copy-done.1) | copy-start | bytes 5898244
  132.3 1.2 copy-start.12
  133.6 1.0 copy-start.13
  133.6 1.1 copy-start.15
  133.6 1.1 copy-start.16
  133.6 1.2 copy-start.17
  139.6 6.8 %copy-start.7 = (f32[5,3,4,64,128]{4,3,2,1,0:T(8,128)}, f32[5,3,4,64,128]{4,3,2,1,0:T(8,128)S(1)}, u32[]{:S(2)}) copy-start(f32[5,3,4,64,128]{4,3,2,1,0:T(8,128)S(1)} %broadcast_multiply_fusion) | copy-start | bytes 5898244
  224.6 7.0 %copy-start.20 = (f32[1,4]{1,0:T(1,128)}, f32[1,4]{1,0:T(1,128)S(1)}, u32[]{:S(2)}) copy-start(f32[1,4]{1,0:T(1,128)S(1)} %fusion.25) | copy-start | bytes 52
  231.6 1.3 slice-start
where the time goes:
time: 236 us; the launch traced here: 235 us
  blocking collectives  68.4 us (29%)
  waiting for transfers between devices  52.6 us (22%)
  local copies, waits for them, and re-layouts  47.2 us (20%)
  other arithmetic  42 us (18%)
  matrix products  13.9 us (6%)
  starting transfers between devices  10.3 us (4%)
    psum x1, blocking collectives, per_device(): lax.psum((gram_local, second_local), ('gx', 'gy'))  68.4 us
    ppermute x4, waiting for transfers between devices, padded_2(): lax.ppermute(head, axis, [((i + 1) % count, i) for i in range(count)])  43.9 us
    unnamed x48, local copies, waits for them, and re-layouts  21.9 us
    concatenate x4, other arithmetic, padded_2(): jnp.concatenate([lax.ppermute(tail, axis, [(i, (i + 1) % count) for i in...  14.9 us
    ppermute x4, starting transfers between devices, padded_2(): lax.ppermute(head, axis, [((i + 1) % count, i) for i in range(count)])  8.91 us
    ppermute x4, waiting for transfers between devices, padded_2(): lax.ppermute(tail, axis, [(i, (i + 1) % count) for i in range(count)])  8.67 us
    slice x2, local copies, waits for them, and re-layouts, padded_2(): lax.slice_in_dim(cells, cells.shape[dim] - width, cells.shape[dim], axis=...  8.16 us
    dot_general x1, matrix products, per_device(): gram_local = jnp.dot(matrix, matrix.T, precision=highest)  6.8 us
  transfers between devices with their start and end apart: 8, of which 6 were waited for; matrix products, arithmetic and copies ran while one was open for 6% of the time, Pallas kernels for 0%

commit v1 on v0

--- a/solution.py
+++ b/solution.py
@@ -100,7 +100,7 @@
         local_shape[2] * local_shape[3] * local_shape[4] * lax.axis_size("gx") * lax.axis_size("gy")
     )
     first_total = lax.psum(first_local, ("gx", "gy"))
-    gram_total, carried_total = lax.psum((gram_local, second_local), ("gx", "gy"))
+    gram_total, carried_total = lax.psum(lax.psum((gram_local, second_local), "gx"), "gy")
     objective = 0.5 * (first_total + carried_total) / total_cells
     gram_matrix = gram_total / (3.0 * total_cells)
     lower_factor = jnp.linalg.cholesky(gram_matrix[:4, :4])

time: 236 us -> 287 us (1.22)
  blocking collectives: 68.4 us -> 122 us
    psum x1 -> x3, blocking collectives: 68.4 us -> 122 us  [the longest x1 70.3 us: per_device(): first_total = lax.psum(first_local, ('gx', 'gy'))]
    unnamed x48 -> x50, local copies, waits for them, and re-layouts: 21.9 us -> 21.9 us
  transfers between devices with their start and end apart: 8 -> 8, of which waited for: 6 -> 5; matrix products, arithmetic and copies ran while one was open for 6% -> 5% of each run, Pallas kernels for 0% -> 0%
where the time goes in v1:
time: 287 us; the launch traced here: 286 us
  blocking collectives  122 us (43%)
  waiting for transfers between devices  50.1 us (17%)
  local copies, waits for them, and re-layouts  47.3 us (16%)
  other arithmetic  42.1 us (15%)
  matrix products  13.9 us (5%)
  starting transfers between devices  10.3 us (4%)
    psum x1, blocking collectives, per_device(): first_total = lax.psum(first_local, ('gx', 'gy'))  70.3 us
    ppermute x4, waiting for transfers between devices, padded_2(): lax.ppermute(head, axis, [((i + 1) % count, i) for i in range(count)])  43.9 us
    psum x1, blocking collectives, per_device(): lax.psum(lax.psum((gram_local, second_local), 'gx'), 'gy')  37.3 us
    unnamed x50, local copies, waits for them, and re-layouts  21.9 us
    concatenate x4, other arithmetic, padded_2(): jnp.concatenate([lax.ppermute(tail, axis, [(i, (i + 1) % count) for i in...  14.9 us
    psum x1, blocking collectives, per_device(): lax.psum((gram_local, second_local), 'gx')  13.9 us
    ppermute x4, starting transfers between devices, padded_2(): lax.ppermute(head, axis, [((i + 1) % count, i) for i in range(count)])  8.91 us
    slice x2, local copies, waits for them, and re-layouts, padded_2(): lax.slice_in_dim(cells, cells.shape[dim] - width, cells.shape[dim], axis=...  8.13 us
  transfers between devices with their start and end apart: 8, of which 5 were waited for; matrix products, arithmetic and copies ran while one was open for 5% of the time, Pallas kernels for 0%

profile of v1, /device:TPU:1, one launch (start us, length us, event | category | flops | bytes accessed | tf_op | source)
XLA Modules:
  0.0 286.2 jit_solution(10850259613232999388)
XLA Ops:
  0.6 1.2 slice_bitcast_fusion.7
  1.8 1.4 pad_maximum_fusion.8
  3.3 4.7 %collective-permute-start.1 = (f32[18,1,64,128]{3,2,1,0:T(8,128)S(1)}, f32[18,1,64,128]{3,2,1,0:T(8,128)S(1)}, u32[]{:S(2)}, u32[]{:S(2)}) collective-permute-start(f32[18,1,64,128]{3,2,1,0:T(8,128)S(1)} %get-tuple-element.59), channel_id=1, source_target_pairs={{16,0},{32,16},{48,32},{64,48},{80,64},{96,80},{112,96},{0,112},{1... | collective-permute-start | bytes 1769480 | tf_op jit(solution)/shard_map/ppermute | solution.py:19
  8.0 0.9 multiply_bitcast_fusion.2
  8.9 22.6 %collective-permute-done.1 = f32[18,1,64,128]{3,2,1,0:T(8,128)S(1)} collective-permute-done((f32[18,1,64,128]{3,2,1,0:T(8,128)S(1)}, f32[18,1,64,128]{3,2,1,0:T(8,128)S(1)}, u32[]{:S(2)}, u32[]{:S(2)}) %collective-permute-start.1) | collective-permute-done | bytes 589856 | tf_op jit(solution)/shard_map/ppermute | solution.py:19
  31.5 0.9 collective-permute-done
  32.4 0.8 copy-done.8
  33.2 0.3 pad_maximum_fusion.2
  33.5 4.1 %fusion.32 = (f32[18,6,64,1]{3,2,1,0:T(8,128)}, f32[18,6,64,1]{3,2,1,0:T(8,128)}) fusion(f32[18,6,64,128]{3,2,1,0:T(8,128)S(1)} %pad_maximum_fusion.2), kind=kLoop, calls=%fused_computation.119 | loop fusion | bytes 110592 | tf_op jit(solution)/shard_map/slice | solution.py:14
  37.6 3.0 %copy.69 = f32[18,6,64,1]{2,1,3,0:T(8,128)S(1)} copy(f32[18,6,64,1]{3,2,1,0:T(8,128)} %get-tuple-element.55) | data formatting | bytes 55296
  40.6 0.6 collective-permute-start.3
  41.2 3.6 %copy.68 = f32[18,6,64,1]{2,1,3,0:T(8,128)} copy(f32[18,6,64,1]{3,2,1,0:T(8,128)} %get-tuple-element.54) | data formatting | bytes 55296
  44.8 1.3 collective-permute-start.2
  46.0 3.2 %copy.52 = f32[18,6,64,1]{3,2,1,0:T(8,128)} copy(f32[18,6,64,1]{2,1,3,0:T(8,128)} %collective-permute-done.3) | data formatting | bytes 55296 | tf_op jit(solution)/shard_map/ppermute | solution.py:19
  49.2 2.3 collective-permute-done.2
  51.5 3.2 %copy.51 = f32[18,6,64,1]{3,2,1,0:T(8,128)} copy(f32[18,6,64,1]{2,1,3,0:T(8,128)} %collective-permute-done.2) | data formatting | bytes 55296 | tf_op jit(solution)/shard_map/ppermute | solution.py:17
  54.7 7.0 %pad_maximum_fusion = f32[18,6,64,130]{3,2,1,0:T(8,128)S(1)} fusion(f32[18,6,64,1]{3,2,1,0:T(8,128)} %copy.52, f32[18,1,64,128]{3,2,1,0:T(8,128)S(1)} %collective-permute-done.1, f32[3,4,64,128]{3,2,1,0:T(8,128)S(1)} %get-tuple-element.70, f32[15,4,64,128]{3,2,1,0:T(8,128)S(1)} %bitcast.73, f32[18,1,64,128]{3,2,1,0:T(8,128)} %copy-done.8, f32[18,6,64,1]{3,2,1,0:T(8,128)} %copy.51), kind=kLoop, calls=%fused_computation | loop fusion | flops 4492800 | bytes 7188480 | tf_op jit(solution)/shard_map/concatenate | solution.py:15
  61.8 0.7 slice.409
  62.5 0.6 slice_bitcast_fusion.5
  63.1 0.7 copy-done.5
  63.9 1.3 copy-done.3
  65.2 0.6 select_maximum_fusion.5
  65.8 0.5 subtract_multiply_fusion.5
  66.3 0.6 copy-done.11
  67.0 0.3 subtract_multiply_fusion.3
  67.4 3.8 %multiply_reduce_fusion.1 = (f32[5]{0:T(128)S(1)}, f32[5,3,4,64,128]{4,3,2,1,0:T(8,128)S(1)}) fusion(f32[3,4,64,128]{3,2,1,0:T(8,128)S(1)} %copy-done.14, f32[5,3,4,64,128]{4,3,2,1,0:T(8,128)S(1)} %copy-done, f32[3,4,64,128]{3,2,1,0:T(8,128)S(1)} %get-tuple-element.63, f32[5]{0:T(128)S(1)} %compare_convert_fusion, f32[5,3,6,64,130]{4,3,2,1,0:T(8,128)S(1)} %bitcast.84, ...), kind=kLoop, calls=%fused_computation.28 | loop fusion | flops 14745595 | bytes 23986708 | tf_op jit(solution)/shard_map/reduce_sum | solution.py:95
  71.4 2.0 collective-permute-start.5
  73.4 0.8 broadcast_multiply_fusion.1
  74.2 21.3 %collective-permute-done.5 = f32[18,1,64,128]{3,2,1,0:T(8,128)S(1)} collective-permute-done((f32[18,1,64,128]{3,2,1,0:T(8,128)S(1)}, f32[18,1,64,128]{3,2,1,0:T(8,128)S(1)}, u32[]{:S(2)}, u32[]{:S(2)}) %collective-permute-start.5) | collective-permute-done | bytes 589856 | tf_op jit(solution)/shard_map/ppermute | solution.py:19
  95.5 2.9 %collective-permute-done.4 = f32[18,1,64,128]{3,2,1,0:T(8,128)S(1)} collective-permute-done((f32[18,1,64,128]{3,2,1,0:T(8,128)S(1)}, f32[18,1,64,128]{3,2,1,0:T(8,128)S(1)}, u32[]{:S(2)}, u32[]{:S(2)}) %collective-permute-start.4) | collective-permute-done | bytes 589856 | tf_op jit(solution)/shard_map/ppermute | solution.py:17
  98.4 0.4 pad_maximum_fusion.3
  98.8 4.1 %fusion.31 = (f32[18,6,64,1]{3,2,1,0:T(8,128)}, f32[18,6,64,1]{3,2,1,0:T(8,128)}) fusion(f32[18,6,64,128]{3,2,1,0:T(8,128)S(1)} %pad_maximum_fusion.3), kind=kLoop, calls=%fused_computation.118 | loop fusion | bytes 110592 | tf_op jit(solution)/shard_map/slice | solution.py:14
  102.8 3.6 %copy.71 = f32[18,6,64,1]{2,1,3,0:T(8,128)} copy(f32[18,6,64,1]{3,2,1,0:T(8,128)} %get-tuple-element.50) | data formatting | bytes 55296
  106.4 1.6 collective-permute-start.7
  108.0 3.6 %copy.70 = f32[18,6,64,1]{2,1,3,0:T(8,128)} copy(f32[18,6,64,1]{3,2,1,0:T(8,128)} %get-tuple-element.49) | data formatting | bytes 55296
  111.8 70.3 %psum.37 = f32[5]{0:T(128)} all-reduce(f32[5]{0:T(128)S(1)} %get-tuple-element.20), channel_id=1, replica_groups=mesh['gx'=8,'gy'=16] {'gx','gy'}, use_global_device_ids=true, to_apply=%region_5.6 | all-reduce | flops 5 | bytes 40 | tf_op jit(solution)/shard_map/psum | solution.py:102
  182.1 3.2 %copy.58 = f32[18,6,64,1]{3,2,1,0:T(8,128)} copy(f32[18,6,64,1]{2,1,3,0:T(8,128)} %collective-permute-done.7) | data formatting | bytes 55296 | tf_op jit(solution)/shard_map/ppermute | solution.py:19
  185.3 3.2 %copy.57 = f32[18,6,64,1]{3,2,1,0:T(8,128)} copy(f32[18,6,64,1]{2,1,3,0:T(8,128)} %collective-permute-done.6) | data formatting | bytes 55296 | tf_op jit(solution)/shard_map/ppermute | solution.py:17
  188.5 7.2 %pad_maximum_fusion.1 = f32[18,6,64,130]{3,2,1,0:T(8,128)S(1)} fusion(f32[18,6,64,1]{3,2,1,0:T(8,128)} %copy.58, f32[18,1,64,128]{3,2,1,0:T(8,128)S(1)} %collective-permute-done.5, f32[3,4,64,128]{3,2,1,0:T(8,128)S(1)} %get-tuple-element.71, f32[15,4,64,128]{3,2,1,0:T(8,128)} %bitcast.78, f32[18,1,64,128]{3,2,1,0:T(8,128)S(1)} %collective-permute-done.4, ...), kind=kLoop, calls=%fused_computation.1 | loop fusion | flops 4492800 | bytes 7188480 | tf_op jit(solution)/shard_map/concatenate | solution.py:15
  195.7 0.4 slice.422
  196.1 0.6 slice_bitcast_fusion.2
  196.7 1.0 copy-done.4
  197.7 1.1 copy-done.6
  198.8 0.7 copy-done.2
  199.4 0.6 select_maximum_fusion
  200.0 1.2 subtract_multiply_fusion.2
  201.3 0.3 subtract_multiply_fusion
  201.6 0.6 copy-done.13
  202.4 4.9 %multiply_reduce_fusion = (f32[5]{0:T(128)S(1)}, f32[5,3,4,64,128]{4,3,2,1,0:T(8,128)S(1)}) fusion(f32[3,4,64,128]{3,2,1,0:T(8,128)S(1)} %copy-done.15, f32[3,4,64,128]{3,2,1,0:T(8,128)S(1)} %get-tuple-element.61, f32[5]{0:T(128)S(1)} %compare_convert_fusion, f32[5,3,6,64,130]{4,3,2,1,0:T(8,128)S(1)} %bitcast.82, ...), kind=kLoop, calls=%fused_computation.27 | loop fusion | flops 15237115 | bytes 25952788 | tf_op jit(solution)/shard_map/reduce_sum | solution.py:96
  207.6 6.8 %fusion.18 = f32[5,5]{0,1:T(8,128)S(1)} fusion(f32[5,3,4,64,128]{4,3,2,1,0:T(8,128)S(1)} %broadcast_multiply_fusion), kind=kOutput, calls=%fused_computation.43 | convolution fusion | flops 29491200 | bytes 1966180 | tf_op jit(solution)/shard_map/dot_general | solution.py:98
  214.4 13.9 %all-reduce.5 = (f32[5,5]{0,1:T(8,128)S(1)}, f32[5]{0:T(128)S(1)}) all-reduce(f32[5,5]{0,1:T(8,128)S(1)} %fusion.18, f32[5]{0:T(128)S(1)} %get-tuple-element.26), channel_id=1, replica_groups=mesh['gx'=8,'gy'=16] {'gx'}, use_global_device_ids=true, to_apply=%region_0.1 | all-reduce | flops 30 | bytes 240 | tf_op jit(solution)/shard_map/psum | solution.py:103
  228.4 37.3 %all-reduce.4 = (f32[5,5]{0,1:T(8,128)S(1)}, f32[5]{0:T(128)S(1)}) all-reduce(f32[5,5]{0,1:T(8,128)S(1)} %get-tuple-element.18, f32[5]{0:T(128)S(1)} %get-tuple-element.19), channel_id=1, replica_groups=mesh['gx'=8,'gy'=16] {'gy'}, use_global_device_ids=true, to_apply=%region_1.2 | all-reduce | flops 30 | bytes 240 | tf_op jit(solution)/shard_map/psum | solution.py:103
  265.8 0.4 cholesky.14
  266.2 0.6 compare_reduce_fusion
  266.9 0.6 select_select_fusion
  267.5 0.7 fusion.35
  268.2 0.7 fusion.33
  268.8 6.2 %subtract_divide_fusion = (f32[1,4]{1,0:T(1,128)S(1)}, f32[1,4]{1,0:T(1,128)S(1)}, f32[1,4]{1,0:T(1,128)S(1)}, f32[1,4]{1,0:T(1,128)S(1)}) fusion(f32[4,4]{1,0:T(4,128)S(1)} %fusion.22, f32[]{:T(128)} %bitcast.29, f32[]{:T(128)} %bitcast.28, f32[]{:T(128)} %bitcast.27, f32[]{:T(128)} %bitcast.26, f32[]{:T(128)} %bitcast.25, f32[]{:T(128)} %bitcast.24, ...), kind=kLoop, calls=%fused_computation.110 | loop fusion | flops 64 | bytes 168 | tf_op jit(solution)/shard_map/div | solution.py:82
  275.2 3.5 %fusion.14 = f32[4,98304]{1,0:T(4,128)S(1)} fusion(f32[1,4,768,128]{3,2,1,0:T(8,128)S(1)} %bitcast.87, f32[1,4]{1,0:T(1,128)S(1)} %get-tuple-element.22, f32[1,4]{1,0:T(1,128)S(1)} %get-tuple-element.23, f32[1,4]{1,0:T(1,128)S(1)} %get-tuple-element.24, f32[1,4]{1,0:T(1,128)S(1)} %get-tuple-element.25), kind=kOutput, calls=%fused_computation.29 | convolution fusion | flops 18874416 | bytes 3145792 | tf_op jit(solution)/shard_map/dot_general | solution.py:109
  278.8 3.4 %fusion.23 = f32[1,98304]{1,0:T(1,128)} fusion(f32[4,98304]{1,0:T(4,128)S(1)} %fusion.14, f32[1,4]{1,0:T(1,128)S(1)} %fusion.25), kind=kOutput, calls=%fused_computation.107 | convolution fusion | flops 4718592 | bytes 1966096 | tf_op jit(solution)/shard_map/dot_general | solution.py:110
  282.3 0.7 copy.65
  283.2 1.0 sub.109
  284.3 1.4 pad_maximum_fusion.4
  285.7 0.5 add_multiply_fusion
  (56 shorter events, 1.7 us)
Async XLA Ops:
  1.8 6.2 %copy-start.10 = (f32[2,3,4,64,128]{4,3,2,1,0:T(8,128)S(1)}, f32[2,3,4,64,128]{4,3,2,1,0:T(8,128)}, u32[]{:S(2)}) copy-start(f32[2,3,4,64,128]{4,3,2,1,0:T(8,128)} %param.4) | copy-start | bytes 2359300
  1.8 31.4 %copy-start = (f32[5,3,4,64,128]{4,3,2,1,0:T(8,128)S(1)}, f32[5,3,4,64,128]{4,3,2,1,0:T(8,128)}, u32[]{:S(2)}) copy-start(f32[5,3,4,64,128]{4,3,2,1,0:T(8,128)} %param.3) | copy-start | bytes 5898244
  3.3 28.2 %collective-permute-start.1 = (f32[18,1,64,128]{3,2,1,0:T(8,128)S(1)}, f32[18,1,64,128]{3,2,1,0:T(8,128)S(1)}, u32[]{:S(2)}, u32[]{:S(2)}) collective-permute-start(f32[18,1,64,128]{3,2,1,0:T(8,128)S(1)} %get-tuple-element.59), channel_id=1, source_target_pairs={{16,0},{32,16},{48,32},{64,48},{80,64},{96,80},{112,96},{0,112},{1... | collective-permute-start | bytes 1769480 | tf_op jit(solution)/shard_map/ppermute | solution.py:19
  8.0 24.4 %collective-permute-start = (f32[18,1,64,128]{3,2,1,0:T(8,128)S(1)}, f32[18,1,64,128]{3,2,1,0:T(8,128)S(1)}, u32[]{:S(2)}, u32[]{:S(2)}) collective-permute-start(f32[18,1,64,128]{3,2,1,0:T(8,128)S(1)} %get-tuple-element.58), channel_id=1, source_target_pairs={{0,16},{16,32},{32,48},{48,64},{64,80},{80,96},{96,112},{112,0},{1... | collective-permute-start | bytes 1769480 | tf_op jit(solution)/shard_map/ppermute | solution.py:17
  32.4 0.8 copy-start.8
  40.6 5.4 %collective-permute-start.3 = (f32[18,6,64,1]{2,1,3,0:T(8,128)S(1)}, f32[18,6,64,1]{2,1,3,0:T(8,128)}, u32[]{:S(2)}, u32[]{:S(2)}) collective-permute-start(f32[18,6,64,1]{2,1,3,0:T(8,128)S(1)} %copy.69), channel_id=1, source_target_pairs={{1,0},{2,1},{3,2},{4,3},{5,4},{6,5},{7,6},{8,7},{9,8},{10,9},{11,1... | collective-permute-start | bytes 82952 | tf_op jit(solution)/shard_map/ppermute | solution.py:19
  44.8 6.8 %collective-permute-start.2 = (f32[18,6,64,1]{2,1,3,0:T(8,128)}, f32[18,6,64,1]{2,1,3,0:T(8,128)}, u32[]{:S(2)}, u32[]{:S(2)}) collective-permute-start(f32[18,6,64,1]{2,1,3,0:T(8,128)} %copy.68), channel_id=1, source_target_pairs={{0,1},{1,2},{2,3},{3,4},{4,5},{5,6},{6,7},{7,8},{8,9},{9,10},{10,1... | collective-permute-start | bytes 82952 | tf_op jit(solution)/shard_map/ppermute | solution.py:17
  61.8 2.0 copy-start.5
  61.8 2.1 copy-start.9
  62.5 2.7 copy-start.3
  65.8 1.1 copy-start.11
  66.3 1.1 copy-start.14
  66.3 1.1 copy-start.18
  66.3 1.1 copy-start.19
  71.3 27.1 %copy-start.1 = (f32[5,3,4,64,128]{4,3,2,1,0:T(8,128)}, f32[5,3,4,64,128]{4,3,2,1,0:T(8,128)S(1)}, u32[]{:S(2)}) copy-start(f32[5,3,4,64,128]{4,3,2,1,0:T(8,128)S(1)} %get-tuple-element.21) | copy-start | bytes 5898244
  71.4 24.1 %collective-permute-start.5 = (f32[18,1,64,128]{3,2,1,0:T(8,128)S(1)}, f32[18,1,64,128]{3,2,1,0:T(8,128)S(1)}, u32[]{:S(2)}, u32[]{:S(2)}) collective-permute-start(f32[18,1,64,128]{3,2,1,0:T(8,128)S(1)} %get-tuple-element.57), channel_id=1, source_target_pairs={{16,0},{32,16},{48,32},{64,48},{80,64},{96,80},{112,96},{0,112},{1... | collective-permute-start | bytes 1769480 | tf_op jit(solution)/shard_map/ppermute | solution.py:19
  73.4 25.0 %collective-permute-start.4 = (f32[18,1,64,128]{3,2,1,0:T(8,128)S(1)}, f32[18,1,64,128]{3,2,1,0:T(8,128)S(1)}, u32[]{:S(2)}, u32[]{:S(2)}) collective-permute-start(f32[18,1,64,128]{3,2,1,0:T(8,128)S(1)} %get-tuple-element.56), channel_id=1, source_target_pairs={{0,16},{16,32},{32,48},{48,64},{64,80},{80,96},{96,112},{112,0},{1... | collective-permute-start | bytes 1769480 | tf_op jit(solution)/shard_map/ppermute | solution.py:17
  106.4 75.6 %collective-permute-start.7 = (f32[18,6,64,1]{2,1,3,0:T(8,128)}, f32[18,6,64,1]{2,1,3,0:T(8,128)}, u32[]{:S(2)}, u32[]{:S(2)}) collective-permute-start(f32[18,6,64,1]{2,1,3,0:T(8,128)} %copy.71), channel_id=1, source_target_pairs={{1,0},{2,1},{3,2},{4,3},{5,4},{6,5},{7,6},{8,7},{9,8},{10,9},{11,1... | collective-permute-start | bytes 82952 | tf_op jit(solution)/shard_map/ppermute | solution.py:19
  111.6 73.6 %collective-permute-start.6 = (f32[18,6,64,1]{2,1,3,0:T(8,128)}, f32[18,6,64,1]{2,1,3,0:T(8,128)}, u32[]{:S(2)}, u32[]{:S(2)}) collective-permute-start(f32[18,6,64,1]{2,1,3,0:T(8,128)} %copy.70), channel_id=1, source_target_pairs={{0,1},{1,2},{2,3},{3,4},{4,5},{5,6},{6,7},{7,8},{8,9},{9,10},{10,1... | collective-permute-start | bytes 82952 | tf_op jit(solution)/shard_map/ppermute | solution.py:17
  195.7 2.0 copy-start.4
  195.7 3.1 %copy-start.6 = (f32[18,6,64,1]{3,2,1,0:T(8,128)S(1)}, f32[18,6,64,1]{3,2,1,0:T(8,128)}, u32[]{:S(2)}) copy-start(f32[18,6,64,1]{3,2,1,0:T(8,128)} %copy.57) | copy-start | bytes 82948
  196.1 3.3 %copy-start.2 = (f32[5,3,4,64,128]{4,3,2,1,0:T(8,128)S(1)}, f32[5,3,4,64,128]{4,3,2,1,0:T(8,128)}, u32[]{:S(2)}) copy-start(f32[5,3,4,64,128]{4,3,2,1,0:T(8,128)} %copy-done.1) | copy-start | bytes 5898244
  200.0 1.2 copy-start.12
  201.2 1.0 copy-start.13
  201.2 1.1 copy-start.15
  201.2 1.1 copy-start.16
  201.2 1.2 copy-start.17
  207.5 6.9 %copy-start.7 = (f32[5,3,4,64,128]{4,3,2,1,0:T(8,128)}, f32[5,3,4,64,128]{4,3,2,1,0:T(8,128)S(1)}, u32[]{:S(2)}) copy-start(f32[5,3,4,64,128]{4,3,2,1,0:T(8,128)S(1)} %broadcast_multiply_fusion) | copy-start | bytes 5898244
  275.2 7.0 %copy-start.20 = (f32[1,4]{1,0:T(1,128)}, f32[1,4]{1,0:T(1,128)S(1)}, u32[]{:S(2)}) copy-start(f32[1,4]{1,0:T(1,128)S(1)} %fusion.25) | copy-start | bytes 52
  282.2 1.0 slice-start
  284.3 1.4 copy-start.21
